TPU v7x, 32 devices: a whole 2x2x4 slice. The times are simulated.
32 devices in a mesh: frames: 2 (over x), slabs: 16 (over z, y, core).
Axes of the slice: x: 2, y: 2, z: 4, core: 2. Of those that a mesh axis runs over, the one named last changes fastest.
Arguments:
- movie: bfloat16 [16, 32768], P('frames', 'slabs'), may hold values from -48 to 48
- traces: bfloat16 [16, 256], P('frames', 'slabs'), may hold values from -6 to 6
- voxel_index: int32 [256, 2048], P('slabs'), may hold values from 0 to 4095, as said below
- footprint: float32 [256, 2048], P('slabs'), may hold values from 0 to 1
- block_order: int32 [2], replicated, may hold values from 0 to 1, each once
Outputs:
- updated: float32 [256, 2048], P('slabs')
Inputs may be any that keep to these rules, and one draw needn't show every extreme that they name: `voxel_index`: within a row all 2048 positions are distinct and lie in a run of 4096 consecutive positions, whose first and last position are both in the row.
All inputs are finite; a program needn't handle non-finite values.
Results may differ from a plain program's by a relative error of at most 0.0003.
Values may be sent and summed in bfloat16 or wider, within the bound.
A program may use at most 64 MiB of HBM per device.

v0:
```python
import functools

import jax
import jax.numpy as jnp
from jax import lax
from jax.experimental import pallas as pl
from jax.experimental.pallas import tpu as pltpu
from jax.sharding import PartitionSpec as P

BLOCK = 8
LANES = 128
MESH = pl.DeviceIdType.MESH
F32 = jnp.float32
BF16 = jnp.bfloat16


def dot_nt(left, right):
    return lax.dot_general(left, right, (((1,), (1,)), ((), ())), preferred_element_type=F32)


def dot_nn(left, right):
    return lax.dot_general(left, right, (((1,), (0,)), ((), ())), preferred_element_type=F32)


def halves(value):
    high = value.astype(BF16)
    low = (value - high.astype(F32)).astype(BF16)
    return high, low


def kernel(
    nf, ns, order_in, movie_in, traces_in, index_in, foot_in, out_ref,
    order_ref, movie_ref, traces_ref, index_ref, foot_ref, own, left, right, dense, near,
    hi_s, lo_s, vh_s, vl_s, movie_s, w_s, c_s, inv_s,
    load_sem, send_m, recv_m, send_d, recv_d,
):
    f = lax.axis_index("frames")
    s = lax.axis_index("slabs")
    has_l = s > 0
    has_r = s < ns - 1
    frames, voxels = movie_ref.shape
    margin = voxels // 2
    extent = 2 * voxels
    chunks = extent // LANES
    half = chunks // 2
    foot_n = foot_ref.shape[1]

    barrier = pltpu.get_barrier_semaphore()
    for d in range(1, nf):
        pl.semaphore_signal(barrier, inc=1, device_id=(lax.rem(f + d, nf), s), device_id_type=MESH)

    @pl.when(has_l)
    def _():
        for d in range(nf):
            pl.semaphore_signal(
                barrier, inc=1, device_id=(lax.rem(f + d, nf), s - 1), device_id_type=MESH)

    @pl.when(has_r)
    def _():
        for d in range(nf):
            pl.semaphore_signal(
                barrier, inc=1, device_id=(lax.rem(f + d, nf), s + 1), device_id_type=MESH)

    pairs = ((index_in, index_ref), (foot_in, foot_ref), (order_in, order_ref),
             (movie_in, movie_ref), (traces_in, traces_ref))
    loads = [pltpu.make_async_copy(a, b, load_sem.at[i]) for i, (a, b) in enumerate(pairs)]
    for load in loads:
        load.start()

    loads[3].wait()
    loads[4].wait()
    quarter = margin // 2
    parts = movie_ref[...].astype(F32)
    for h, at in ((0, 0), (1, quarter + LANES)):
        own[f, :, at:at + quarter] = jnp.concatenate(
            [parts[:, 2 * h * quarter:(2 * h + 1) * quarter],
             parts[:, (2 * h + 1) * quarter:(2 * h + 2) * quarter]], axis=0).astype(BF16)
    lead = jnp.concatenate(
        [traces_ref[...].astype(F32), jnp.zeros((frames, LANES - 2 * BLOCK), F32)], axis=1)
    own[f, :, quarter:quarter + LANES] = jnp.concatenate(
        [lead, jnp.zeros((frames, LANES), F32)], axis=0).astype(BF16)

    @pl.when(jnp.logical_not(has_l))
    def _():
        left[...] = jnp.zeros_like(left)
        near[0] = jnp.full(near.shape[1:], -1.0, F32)

    @pl.when(jnp.logical_not(has_r))
    def _():
        right[...] = jnp.zeros_like(right)
        near[1] = jnp.full(near.shape[1:], -1.0, F32)

    for load in loads[:3]:
        load.wait()
    swap = order_ref[0] != 0

    def permuted(ref):
        a = ref[0:BLOCK, :]
        b = ref[BLOCK:2 * BLOCK, :]
        return jnp.concatenate([jnp.where(swap, b, a), jnp.where(swap, a, b)], axis=0)

    index = permuted(index_ref)
    value = permuted(foot_ref)
    hi_s[...] = (index >> 7).astype(F32)
    lo_s[...] = (index & (LANES - 1)).astype(F32)
    v_hi = value.astype(BF16).astype(F32)
    vl_s[...] = value - v_hi
    vh_s[...] = jnp.where(v_hi == 0.0, -1.0, v_hi)

    def peer(d):
        to = lax.rem(f + d, nf)
        return pltpu.make_async_remote_copy(
            src_ref=own.at[f], dst_ref=own.at[f], send_sem=send_m.at[0, to],
            recv_sem=recv_m.at[0, f], device_id=(to, s), device_id_type=MESH)

    def to_right(d):
        to = lax.rem(f + d, nf)
        return pltpu.make_async_remote_copy(
            src_ref=own.at[f, :, pl.ds(quarter, quarter + LANES)], dst_ref=left.at[f],
            send_sem=send_m.at[1, to], recv_sem=recv_m.at[1, f],
            device_id=(to, s + 1), device_id_type=MESH)

    def to_left(d):
        to = lax.rem(f + d, nf)
        return pltpu.make_async_remote_copy(
            src_ref=own.at[f, :, pl.ds(0, quarter + LANES)], dst_ref=right.at[f],
            send_sem=send_m.at[2, to], recv_sem=recv_m.at[2, f],
            device_id=(to, s - 1), device_id_type=MESH)

    rows16 = 2 * BLOCK
    iota = lax.broadcasted_iota(jnp.int32, (rows16, foot_n), 0).astype(F32)
    span = half * BLOCK

    def dense_right(b):
        return pltpu.make_async_remote_copy(
            src_ref=dense.at[2 * b + 1], dst_ref=near.at[0, pl.ds(b * span, span), :],
            send_sem=send_d.at[0, b], recv_sem=recv_d.at[0, b],
            device_id=(f, s + 1), device_id_type=MESH)

    def dense_left(b):
        return pltpu.make_async_remote_copy(
            src_ref=dense.at[2 * b], dst_ref=near.at[1, pl.ds(b * span, span), :],
            send_sem=send_d.at[1, b], recv_sem=recv_d.at[1, b],
            device_id=(f, s - 1), device_id_type=MESH)

    for b in range(2):
        def scatter_row(k, b=b):
            row = pl.ds(b * BLOCK + k, 1)

            def spread(ref):
                return jnp.broadcast_to(ref[row, :], (rows16, foot_n)).astype(BF16)

            hi = spread(hi_s)
            lo = spread(lo_s)
            vh = spread(vh_s)
            vl = spread(vl_s)
            zero = jnp.zeros((rows16, foot_n), BF16)
            one = jnp.ones((rows16, foot_n), BF16)
            iota16 = iota.astype(BF16)
            low = [jnp.where(lo == iota16 + BF16(16 * t), one, zero) for t in range(LANES // 16)]
            high = [hi == iota16 + BF16(16 * t) for t in range(chunks // 16)]
            lhs = [jnp.where(m, vh, zero) for m in high] + [jnp.where(m, vl, zero) for m in high]
            got = dot_nt(jnp.concatenate(lhs, axis=0), jnp.concatenate(low, axis=0))
            g_hi = got[:chunks]
            enc = jnp.where(g_hi == 0.0, -1.0, jnp.maximum(g_hi, 0.0) + got[chunks:])
            dense[2 * b, pl.ds(k, half, stride=BLOCK), :] = enc[:half]
            dense[2 * b + 1, pl.ds(k, half, stride=BLOCK), :] = enc[half:]

        for k in range(BLOCK):
            scatter_row(k)

            if b == 0 and k == BLOCK // 2 - 1:
                count = nf - 1 + nf * has_l.astype(jnp.int32) + nf * has_r.astype(jnp.int32)
                pl.semaphore_wait(barrier, count)

                for d in range(1, nf):
                    peer(d).start()

                @pl.when(has_r)
                def _():
                    for d in range(nf):
                        to_right(d).start()

                @pl.when(has_l)
                def _():
                    for d in range(nf):
                        to_left(d).start()

        @pl.when(has_r)
        def _(b=b):
            dense_right(b).start()

        @pl.when(has_l)
        def _(b=b):
            dense_left(b).start()

    for d in range(1, nf):
        pltpu.make_async_remote_copy(
            src_ref=own.at[f], dst_ref=own.at[lax.rem(f + d, nf)], send_sem=send_m.at[0, 0],
            recv_sem=recv_m.at[0, lax.rem(f + d, nf)], device_id=(f, s),
            device_id_type=MESH).wait_recv()

    @pl.when(has_l)
    def _():
        for d in range(nf):
            pltpu.make_async_remote_copy(
                src_ref=left.at[d], dst_ref=left.at[d], send_sem=send_m.at[1, 0],
                recv_sem=recv_m.at[1, d], device_id=(f, s), device_id_type=MESH).wait_recv()

    @pl.when(has_r)
    def _():
        for d in range(nf):
            pltpu.make_async_remote_copy(
                src_ref=right.at[d], dst_ref=right.at[d], send_sem=send_m.at[2, 0],
                recv_sem=recv_m.at[2, d], device_id=(f, s), device_id_type=MESH).wait_recv()

    def all_frames(pick):
        return jnp.concatenate([pick(g) for g in range(nf)], axis=0)

    def unpacked(ref, at):
        def one(g):
            both = ref[g, :, at:at + quarter].astype(F32)
            return jnp.concatenate([both[:frames], both[frames:]], axis=1)
        return all_frames(one)

    def trace_rows(ref, at):
        return lambda g: ref[g, :, at:at + LANES].astype(F32)[:frames]

    movie_l = jnp.concatenate([unpacked(left, LANES), unpacked(own, 0)], axis=1).astype(BF16)
    movie_r = jnp.concatenate(
        [unpacked(own, quarter + LANES), unpacked(right, 0)], axis=1).astype(BF16)
    total = nf * frames
    padding = jnp.zeros((LANES - total, LANES), F32)
    eye = (lax.broadcasted_iota(jnp.int32, (rows16, LANES), 0)
           == lax.broadcasted_iota(jnp.int32, (rows16, LANES), 1)).astype(F32).astype(BF16)

    def by_source(pick):
        block = jnp.concatenate([all_frames(pick), padding], axis=0).astype(BF16)
        rows = dot_nt(eye, block)
        return jnp.concatenate([jnp.where(swap, rows[BLOCK:], rows[:BLOCK]),
                                jnp.where(swap, rows[:BLOCK], rows[BLOCK:])], axis=0)

    t_own = by_source(trace_rows(own, quarter))
    t_left = by_source(trace_rows(left, 0))
    t_right = by_source(trace_rows(right, quarter))

    depth = -(-(total + 3 * 32) // LANES) * LANES
    identity = (lax.broadcasted_iota(jnp.int32, (total, LANES), 0)
                == lax.broadcasted_iota(jnp.int32, (total, LANES), 1)).astype(F32)

    def weights(t_near):
        t32 = jnp.concatenate([t_own, t_near], axis=0)
        stacked = jnp.concatenate(
            [identity, t32, t32, t32,
             jnp.zeros((depth - total - 96, LANES), F32)], axis=0).astype(BF16)
        full = dot_nt(t32.astype(BF16), stacked)
        lane = lax.broadcasted_iota(jnp.int32, full.shape, 1)
        g_hi = full.astype(BF16).astype(F32)
        picked = jnp.where((lane >= total + 32) & (lane < total + 64), full - g_hi, g_hi)
        first = jnp.where(lane < total, full, -picked).astype(BF16)
        t_f = jnp.concatenate([t32[0:8], t32[16:24]], axis=0)
        t_s = jnp.concatenate([t32[8:16], t32[24:32]], axis=0)
        stacked2 = jnp.concatenate(
            [t_f, t_f, t_f, jnp.zeros((LANES - 48, LANES), F32)], axis=0).astype(BF16)
        cross = dot_nt(t_s.astype(BF16), stacked2)
        lane2 = lax.broadcasted_iota(jnp.int32, cross.shape, 1)
        row2 = lax.broadcasted_iota(jnp.int32, cross.shape, 0)
        c_hi = cross.astype(BF16).astype(F32)
        picked2 = jnp.where((lane2 >= 16) & (lane2 < 32), cross - c_hi, c_hi)
        same = (row2 // 8) == ((lane2 // 8) % 2)
        second = jnp.where(same, picked2, 0.0).astype(BF16)
        inverse = 1.0 / (jnp.sum(t32 * t32, axis=1, keepdims=True) + 1.0)
        return first, second, inverse

    for side, (movie, t_near) in enumerate(((movie_l, t_left), (movie_r, t_right))):
        w, c, inverse = weights(t_near)
        movie_s[side] = movie
        w_s[side] = w
        c_s[side] = c
        inv_s[side] = jnp.broadcast_to(inverse, (4 * BLOCK, LANES))

    tiles = foot_n // LANES
    places = [[index_ref[b * BLOCK:(b + 1) * BLOCK, j * LANES:(j + 1) * LANES]
               for j in range(tiles)] for b in range(2)]
    taken = [[jnp.zeros((BLOCK, LANES), F32)] * tiles for b in range(2)]

    early = 1 - lax.rem(s, 2)
    for side in (early, 1 - early):
        @pl.when(jnp.where(side == 0, s, ns - 1 - s) > 0)
        def _(side=side):
            for b in range(2):
                pltpu.make_async_remote_copy(
                    src_ref=near.at[side, pl.ds(b * span, span), :],
                    dst_ref=near.at[side, pl.ds(b * span, span), :],
                    send_sem=send_d.at[0, 0], recv_sem=recv_d.at[side, b],
                    device_id=(f, s), device_id_type=MESH).wait_recv()

        def wide(ref, at, start):
            return jnp.concatenate(
                [ref[at, (start + c) * BLOCK:(start + c + 1) * BLOCK, :] for c in range(half)],
                axis=1)

        movie = movie_s[side]
        w = w_s[side][:, :total + 96]
        cross = c_s[side][:, :48]
        inverse = inv_s[side][:, 0:1]
        enc = [wide(dense, side, 0), wide(dense, 2 + side, 0),
               wide(near, side, 0), wide(near, side, half)]
        mask = [(e >= 0.0).astype(F32) for e in enc]
        state = [jnp.maximum(e, 0.0) for e in enc]

        def residual(w_rows, state):
            high, low = halves(jnp.concatenate(state, axis=0))
            return dot_nn(w_rows, jnp.concatenate([movie, high, high, low], axis=0))

        def change(c_rows, old, new):
            high, low = halves(jnp.concatenate([n - o for n, o in zip(new, old)], axis=0))
            return dot_nn(c_rows, jnp.concatenate([high, high, low], axis=0))

        def step(i, rest):
            return mask[i] * jnp.maximum(state[i] + rest * inverse[8 * i:8 * i + 8], 0.0)

        rest = residual(w, state)
        new_f = [step(0, rest[0:8]), step(2, rest[16:24])]
        moved = change(cross, [state[0], state[2]], new_f)
        new_s = [step(1, rest[8:16] - moved[0:8]), step(3, rest[24:32] - moved[8:16])]
        state = [new_f[0], new_s[0], new_f[1], new_s[1]]
        rest = residual(w[0:16], state)
        new_f = step(0, rest[0:8])
        moved = change(cross, [state[0], state[2]], [new_f, state[2]])
        new_s = step(1, rest[8:16] - moved[0:8])
        done = (jnp.where(swap, new_s, new_f), jnp.where(swap, new_f, new_s))
        for b in range(2):
            for j in range(tiles):
                chunk = (places[b][j] >> 7) - half * side
                lane = places[b][j] & (LANES - 1)
                for c in range(half):
                    tile = done[b][:, c * LANES:(c + 1) * LANES]
                    got = jnp.take_along_axis(tile, lane, axis=1, mode="promise_in_bounds")
                    taken[b][j] = jnp.where(chunk == c, got, taken[b][j])

    for b in range(2):
        for j in range(tiles):
            out_ref[b * BLOCK:(b + 1) * BLOCK, j * LANES:(j + 1) * LANES] = taken[b][j]

    for d in range(1, nf):
        peer(d).wait_send()

    @pl.when(has_r)
    def _():
        for d in range(nf):
            to_right(d).wait_send()
        for b in range(2):
            dense_right(b).wait_send()

    @pl.when(has_l)
    def _():
        for d in range(nf):
            to_left(d).wait_send()
        for b in range(2):
            dense_left(b).wait_send()


def local(movie, traces, voxel_index, footprint, block_order):
    nf = lax.axis_size("frames")
    ns = lax.axis_size("slabs")
    frames, voxels = movie.shape
    sources, foot_n = footprint.shape
    margin = voxels // 2
    chunks = 2 * voxels // LANES
    depth = -(-(nf * frames + 3 * 32) // LANES) * LANES
    vmem = pl.BlockSpec(memory_space=pltpu.VMEM)
    return pl.pallas_call(
        functools.partial(kernel, nf, ns),
        out_shape=pltpu.VMEM((sources, foot_n), F32),
        in_specs=[pl.BlockSpec(memory_space=pltpu.HBM)] * 5,
        out_specs=vmem,
        scratch_shapes=[
            pltpu.SMEM(block_order.shape, block_order.dtype),
            pltpu.VMEM(movie.shape, movie.dtype),
            pltpu.VMEM(traces.shape, traces.dtype),
            pltpu.VMEM(voxel_index.shape, voxel_index.dtype),
            pltpu.VMEM(footprint.shape, footprint.dtype),
            pltpu.VMEM((nf, 2 * frames, margin + LANES), BF16),
            pltpu.VMEM((nf, 2 * frames, margin // 2 + LANES), BF16),
            pltpu.VMEM((nf, 2 * frames, margin // 2 + LANES), BF16),
            pltpu.VMEM((4, BLOCK * chunks // 2, LANES), F32),
            pltpu.VMEM((2, BLOCK * chunks, LANES), F32),
            pltpu.VMEM((sources, foot_n), F32),
            pltpu.VMEM((sources, foot_n), F32),
            pltpu.VMEM((sources, foot_n), F32),
            pltpu.VMEM((sources, foot_n), F32),
            pltpu.VMEM((2, nf * frames, voxels), BF16),
            pltpu.VMEM((2, 4 * BLOCK, depth), BF16),
            pltpu.VMEM((2, 2 * BLOCK, LANES), BF16),
            pltpu.VMEM((2, 4 * BLOCK, LANES), F32),
            pltpu.SemaphoreType.DMA((5,)),
            pltpu.SemaphoreType.DMA((3, nf)),
            pltpu.SemaphoreType.DMA((3, nf)),
            pltpu.SemaphoreType.DMA((2, 2)),
            pltpu.SemaphoreType.DMA((2, 2)),
        ],
        compiler_params=pltpu.CompilerParams(
            collective_id=0, has_side_effects=True, vmem_limit_bytes=32 * 1024 * 1024),
        cost_estimate=pl.CostEstimate(
            flops=2 * sources * 64 * LANES * foot_n, bytes_accessed=500000, transcendentals=0),
    )(*(pltpu.with_memory_space_constraint(x, pltpu.HBM)
        for x in (block_order, movie, traces, voxel_index, footprint)))


def solution(mesh):
    in_specs = (P("frames", "slabs"), P("frames", "slabs"), P("slabs", None), P("slabs", None), P())
    out_specs = P("slabs", None)
    return jax.shard_map(local, mesh=mesh, in_specs=in_specs, out_specs=out_specs, check_vma=False)
```

profile of v0, /device:TPU:1, one launch (start us, length us, event | category | flops | bytes accessed | tf_op | source)
XLA Modules:
  0.0 11.8 jit_solution(5698180073388378485)
XLA Ops:
  0.0 11.1 %shard_map.55 = f32[16,2048]{1,0:T(8,128)S(1)} custom-call(s32[2]{0:T(128)} %order_in.1, bf16[8,2048]{1,0:T(8,128)(2,1)} %movie_in.1, bf16[8,16]{1,0:T(8,128)(2,1)} %traces_in.1, s32[16,2048]{1,0:T(8,128)} %index_in.1, f32[16,2048]{1,0:T(8,128)} %foot_in.1), custom_call_target="tpu_custom_call" | custom-call | flops 536870912 | bytes 500000 | tf_op jit(solution)/shard_map/pallas_call | solution.py:373
  11.1 0.7 %copy.7 = f32[16,2048]{1,0:T(8,128)} copy(f32[16,2048]{1,0:T(8,128)S(1)} %shard_map.55) | data formatting | bytes 262144
where the time goes:
time: 11.9 us; the launch traced here: 11.8 us
  Pallas kernels  11.1 us (93%)
  local copies, waits for them, and re-layouts  0.66 us (6%)
    pallas_call x1, Pallas kernels, local(): pl.pallas_call(functools.partial(kernel, nf, ns), out_shape=pltpu.VMEM((s...  11.1 us
    unnamed x1, local copies, waits for them, and re-layouts  0.66 us

commit v1 on v0

--- a/solution.py
+++ b/solution.py
@@ -9,6 +9,7 @@
 
 BLOCK = 8
 LANES = 128
+STEPS = 32767.0
 MESH = pl.DeviceIdType.MESH
 F32 = jnp.float32
 BF16 = jnp.bfloat16
@@ -30,8 +31,8 @@
 
 def kernel(
     nf, ns, order_in, movie_in, traces_in, index_in, foot_in, out_ref,
-    order_ref, movie_ref, traces_ref, index_ref, foot_ref, own, left, right, dense, near,
-    hi_s, lo_s, vh_s, vl_s, movie_s, w_s, c_s, inv_s,
+    order_ref, movie_ref, traces_ref, index_ref, foot_ref, own, left, right, dense, sent, near,
+    hi_s, lo_s, vh_s, vl_s, movie_s, w_s, c_s, inv_s, size_s,
     load_sem, send_m, recv_m, send_d, recv_d,
 ):
     f = lax.axis_index("frames")
@@ -75,20 +76,16 @@
         own[f, :, at:at + quarter] = jnp.concatenate(
             [parts[:, 2 * h * quarter:(2 * h + 1) * quarter],
              parts[:, (2 * h + 1) * quarter:(2 * h + 2) * quarter]], axis=0).astype(BF16)
-    lead = jnp.concatenate(
-        [traces_ref[...].astype(F32), jnp.zeros((frames, LANES - 2 * BLOCK), F32)], axis=1)
-    own[f, :, quarter:quarter + LANES] = jnp.concatenate(
-        [lead, jnp.zeros((frames, LANES), F32)], axis=0).astype(BF16)
 
     @pl.when(jnp.logical_not(has_l))
     def _():
         left[...] = jnp.zeros_like(left)
-        near[0] = jnp.full(near.shape[1:], -1.0, F32)
+        near[0] = jnp.full(near.shape[1:], -1, jnp.int32).astype(jnp.int16)
 
     @pl.when(jnp.logical_not(has_r))
     def _():
         right[...] = jnp.zeros_like(right)
-        near[1] = jnp.full(near.shape[1:], -1.0, F32)
+        near[1] = jnp.full(near.shape[1:], -1, jnp.int32).astype(jnp.int16)
 
     for load in loads[:3]:
         load.wait()
@@ -107,6 +104,16 @@
     vl_s[...] = value - v_hi
     vh_s[...] = jnp.where(v_hi == 0.0, -1.0, v_hi)
 
+    largest = jnp.max(value, axis=1, keepdims=True) * 1.01 + 1e-30
+    largest = jnp.broadcast_to(largest, (2 * BLOCK, LANES)).astype(BF16).astype(F32)
+    unit = STEPS / largest
+    lane8 = lax.broadcasted_iota(jnp.int32, (BLOCK, LANES), 1)
+    lead = jnp.concatenate(
+        [traces_ref[...].astype(F32), jnp.zeros((frames, LANES - 2 * BLOCK), F32)], axis=1)
+    own[f, :, quarter:quarter + LANES] = jnp.concatenate(
+        [lead, jnp.where(lane8 < LANES // 2, largest[:BLOCK], largest[BLOCK:])],
+        axis=0).astype(BF16)
+
     def peer(d):
         to = lax.rem(f + d, nf)
         return pltpu.make_async_remote_copy(
@@ -133,13 +140,13 @@
 
     def dense_right(b):
         return pltpu.make_async_remote_copy(
-            src_ref=dense.at[2 * b + 1], dst_ref=near.at[0, pl.ds(b * span, span), :],
+            src_ref=sent.at[2 * b + 1], dst_ref=near.at[0, pl.ds(b * span, span), :],
             send_sem=send_d.at[0, b], recv_sem=recv_d.at[0, b],
             device_id=(f, s + 1), device_id_type=MESH)
 
     def dense_left(b):
         return pltpu.make_async_remote_copy(
-            src_ref=dense.at[2 * b], dst_ref=near.at[1, pl.ds(b * span, span), :],
+            src_ref=sent.at[2 * b], dst_ref=near.at[1, pl.ds(b * span, span), :],
             send_sem=send_d.at[1, b], recv_sem=recv_d.at[1, b],
             device_id=(f, s - 1), device_id_type=MESH)
 
@@ -185,6 +192,11 @@
                 def _():
                     for d in range(nf):
                         to_left(d).start()
+
+        for side in range(2):
+            values = dense[2 * b + side].reshape(half, BLOCK, LANES)
+            steps = jnp.where(values < 0.0, -1.0, values * unit[b * BLOCK:(b + 1) * BLOCK] + 0.5)
+            sent[2 * b + side] = steps.reshape(span, LANES).astype(jnp.int32).astype(jnp.int16)
 
         @pl.when(has_r)
         def _(b=b):
@@ -278,6 +290,11 @@
         w_s[side] = w
         c_s[side] = c
         inv_s[side] = jnp.broadcast_to(inverse, (4 * BLOCK, LANES))
+        block = ((left, 0), (right, quarter))[side]
+        scales = block[0][0, :, block[1]:block[1] + LANES].astype(F32)[frames:] * (1.0 / STEPS)
+        size_s[side] = jnp.concatenate(
+            [jnp.broadcast_to(scales[:, 0:1], (BLOCK, LANES)),
+             jnp.broadcast_to(scales[:, LANES // 2:LANES // 2 + 1], (BLOCK, LANES))], axis=0)
 
     tiles = foot_n // LANES
     places = [[index_ref[b * BLOCK:(b + 1) * BLOCK, j * LANES:(j + 1) * LANES]
@@ -304,8 +321,12 @@
         w = w_s[side][:, :total + 96]
         cross = c_s[side][:, :48]
         inverse = inv_s[side][:, 0:1]
-        enc = [wide(dense, side, 0), wide(dense, 2 + side, 0),
-               wide(near, side, 0), wide(near, side, half)]
+        steps = near[side].astype(jnp.int32).astype(F32).reshape(2, half, BLOCK, LANES)
+        size = size_s[side]
+        enc = [wide(dense, side, 0), wide(dense, 2 + side, 0)]
+        for b in range(2):
+            enc.append(jnp.concatenate(
+                [steps[b, c] * size[b * BLOCK:(b + 1) * BLOCK] for c in range(half)], axis=1))
         mask = [(e >= 0.0).astype(F32) for e in enc]
         state = [jnp.maximum(e, 0.0) for e in enc]
 
@@ -385,7 +406,8 @@
             pltpu.VMEM((nf, 2 * frames, margin // 2 + LANES), BF16),
             pltpu.VMEM((nf, 2 * frames, margin // 2 + LANES), BF16),
             pltpu.VMEM((4, BLOCK * chunks // 2, LANES), F32),
-            pltpu.VMEM((2, BLOCK * chunks, LANES), F32),
+            pltpu.VMEM((4, BLOCK * chunks // 2, LANES), jnp.int16),
+            pltpu.VMEM((2, BLOCK * chunks, LANES), jnp.int16),
             pltpu.VMEM((sources, foot_n), F32),
             pltpu.VMEM((sources, foot_n), F32),
             pltpu.VMEM((sources, foot_n), F32),
@@ -394,6 +416,7 @@
             pltpu.VMEM((2, 4 * BLOCK, depth), BF16),
             pltpu.VMEM((2, 2 * BLOCK, LANES), BF16),
             pltpu.VMEM((2, 4 * BLOCK, LANES), F32),
+            pltpu.VMEM((2, 2 * BLOCK, LANES), F32),
             pltpu.SemaphoreType.DMA((5,)),
             pltpu.SemaphoreType.DMA((3, nf)),
             pltpu.SemaphoreType.DMA((3, nf)),

time: 11.9 us -> 11.9 us (level)
  no operation moved by 1% of the time
where the time goes in v1:
time: 11.9 us; the launch traced here: 11.7 us
  Pallas kernels  11.1 us (93%)
  local copies, waits for them, and re-layouts  0.66 us (6%)
    pallas_call x1, Pallas kernels, local(): pl.pallas_call(functools.partial(kernel, nf, ns), out_shape=pltpu.VMEM((s...  11.1 us
    unnamed x1, local copies, waits for them, and re-layouts  0.66 us

profile of v1, /device:TPU:1, one launch (start us, length us, event | category | flops | bytes accessed | tf_op | source)
XLA Modules:
  0.0 11.7 jit_solution(880320080288074411)
XLA Ops:
  0.0 11.1 %shard_map.55 = f32[16,2048]{1,0:T(8,128)S(1)} custom-call(s32[2]{0:T(128)} %order_in.1, bf16[8,2048]{1,0:T(8,128)(2,1)} %movie_in.1, bf16[8,16]{1,0:T(8,128)(2,1)} %traces_in.1, s32[16,2048]{1,0:T(8,128)} %index_in.1, f32[16,2048]{1,0:T(8,128)} %foot_in.1), custom_call_target="tpu_custom_call" | custom-call | flops 536870912 | bytes 500000 | tf_op jit(solution)/shard_map/pallas_call | solution.py:394
  11.1 0.7 %copy.7 = f32[16,2048]{1,0:T(8,128)} copy(f32[16,2048]{1,0:T(8,128)S(1)} %shard_map.55) | data formatting | bytes 262144

commit v2 on v1

--- a/solution.py
+++ b/solution.py
@@ -32,7 +32,7 @@
 def kernel(
     nf, ns, order_in, movie_in, traces_in, index_in, foot_in, out_ref,
     order_ref, movie_ref, traces_ref, index_ref, foot_ref, own, left, right, dense, sent, near,
-    hi_s, lo_s, vh_s, vl_s, movie_s, w_s, c_s, inv_s, size_s,
+    hi_s, lo_s, vh_s, vl_s, movie_s, w_s, c_s, inv_s, size_s, unit_s,
     load_sem, send_m, recv_m, send_d, recv_d,
 ):
     f = lax.axis_index("frames")
@@ -98,15 +98,18 @@
 
     index = permuted(index_ref)
     value = permuted(foot_ref)
-    hi_s[...] = (index >> 7).astype(F32)
-    lo_s[...] = (index & (LANES - 1)).astype(F32)
     v_hi = value.astype(BF16).astype(F32)
-    vl_s[...] = value - v_hi
-    vh_s[...] = jnp.where(v_hi == 0.0, -1.0, v_hi)
+    for ref, rows in ((hi_s, (index >> 7).astype(F32)),
+                      (lo_s, (index & (LANES - 1)).astype(F32)),
+                      (vl_s, value - v_hi),
+                      (vh_s, jnp.where(v_hi == 0.0, -1.0, v_hi))):
+        ref[0] = rows[:BLOCK]
+        ref[1] = rows[BLOCK:]
 
     largest = jnp.max(value, axis=1, keepdims=True) * 1.01 + 1e-30
     largest = jnp.broadcast_to(largest, (2 * BLOCK, LANES)).astype(BF16).astype(F32)
-    unit = STEPS / largest
+    unit_s[0] = STEPS / largest[:BLOCK]
+    unit_s[1] = STEPS / largest[BLOCK:]
     lane8 = lax.broadcasted_iota(jnp.int32, (BLOCK, LANES), 1)
     lead = jnp.concatenate(
         [traces_ref[...].astype(F32), jnp.zeros((frames, LANES - 2 * BLOCK), F32)], axis=1)
@@ -150,12 +153,11 @@
             send_sem=send_d.at[1, b], recv_sem=recv_d.at[1, b],
             device_id=(f, s - 1), device_id_type=MESH)
 
-    for b in range(2):
-        def scatter_row(k, b=b):
-            row = pl.ds(b * BLOCK + k, 1)
+    def scatter_block(b, carry):
+        def scatter_row(k):
 
             def spread(ref):
-                return jnp.broadcast_to(ref[row, :], (rows16, foot_n)).astype(BF16)
+                return jnp.broadcast_to(ref[b, k:k + 1, :], (rows16, foot_n)).astype(BF16)
 
             hi = spread(hi_s)
             lo = spread(lo_s)
@@ -176,35 +178,41 @@
         for k in range(BLOCK):
             scatter_row(k)
 
-            if b == 0 and k == BLOCK // 2 - 1:
-                count = nf - 1 + nf * has_l.astype(jnp.int32) + nf * has_r.astype(jnp.int32)
-                pl.semaphore_wait(barrier, count)
-
-                for d in range(1, nf):
-                    peer(d).start()
-
-                @pl.when(has_r)
+            if k == BLOCK // 2 - 1:
+                @pl.when(b == 0)
                 def _():
-                    for d in range(nf):
-                        to_right(d).start()
-
-                @pl.when(has_l)
-                def _():
-                    for d in range(nf):
-                        to_left(d).start()
+                    count = nf - 1 + nf * has_l.astype(jnp.int32) + nf * has_r.astype(jnp.int32)
+                    pl.semaphore_wait(barrier, count)
+
+                    for d in range(1, nf):
+                        peer(d).start()
+
+                    @pl.when(has_r)
+                    def _():
+                        for d in range(nf):
+                            to_right(d).start()
+
+                    @pl.when(has_l)
+                    def _():
+                        for d in range(nf):
+                            to_left(d).start()
 
         for side in range(2):
             values = dense[2 * b + side].reshape(half, BLOCK, LANES)
-            steps = jnp.where(values < 0.0, -1.0, values * unit[b * BLOCK:(b + 1) * BLOCK] + 0.5)
+            steps = jnp.where(values < 0.0, -1.0, values * unit_s[b] + 0.5)
             sent[2 * b + side] = steps.reshape(span, LANES).astype(jnp.int32).astype(jnp.int16)
 
         @pl.when(has_r)
-        def _(b=b):
+        def _():
             dense_right(b).start()
 
         @pl.when(has_l)
-        def _(b=b):
+        def _():
             dense_left(b).start()
+
+        return carry
+
+    lax.fori_loop(0, 2, scatter_block, 0)
 
     for d in range(1, nf):
         pltpu.make_async_remote_copy(
@@ -297,14 +305,15 @@
              jnp.broadcast_to(scales[:, LANES // 2:LANES // 2 + 1], (BLOCK, LANES))], axis=0)
 
     tiles = foot_n // LANES
-    places = [[index_ref[b * BLOCK:(b + 1) * BLOCK, j * LANES:(j + 1) * LANES]
-               for j in range(tiles)] for b in range(2)]
-    taken = [[jnp.zeros((BLOCK, LANES), F32)] * tiles for b in range(2)]
+    out_ref[...] = jnp.zeros_like(out_ref)
 
     early = 1 - lax.rem(s, 2)
-    for side in (early, 1 - early):
+
+    def one_side(i, carry):
+        side = jnp.where(i == 0, early, 1 - early)
+
         @pl.when(jnp.where(side == 0, s, ns - 1 - s) > 0)
-        def _(side=side):
+        def _():
             for b in range(2):
                 pltpu.make_async_remote_copy(
                     src_ref=near.at[side, pl.ds(b * span, span), :],
@@ -353,16 +362,19 @@
         done = (jnp.where(swap, new_s, new_f), jnp.where(swap, new_f, new_s))
         for b in range(2):
             for j in range(tiles):
-                chunk = (places[b][j] >> 7) - half * side
-                lane = places[b][j] & (LANES - 1)
+                at = (slice(b * BLOCK, (b + 1) * BLOCK), slice(j * LANES, (j + 1) * LANES))
+                place = index_ref[at]
+                chunk = (place >> 7) - half * side
+                lane = place & (LANES - 1)
+                taken = out_ref[at]
                 for c in range(half):
                     tile = done[b][:, c * LANES:(c + 1) * LANES]
                     got = jnp.take_along_axis(tile, lane, axis=1, mode="promise_in_bounds")
-                    taken[b][j] = jnp.where(chunk == c, got, taken[b][j])
-
-    for b in range(2):
-        for j in range(tiles):
-            out_ref[b * BLOCK:(b + 1) * BLOCK, j * LANES:(j + 1) * LANES] = taken[b][j]
+                    taken = jnp.where(chunk == c, got, taken)
+                out_ref[at] = taken
+        return carry
+
+    lax.fori_loop(0, 2, one_side, 0)
 
     for d in range(1, nf):
         peer(d).wait_send()
@@ -408,15 +420,16 @@
             pltpu.VMEM((4, BLOCK * chunks // 2, LANES), F32),
             pltpu.VMEM((4, BLOCK * chunks // 2, LANES), jnp.int16),
             pltpu.VMEM((2, BLOCK * chunks, LANES), jnp.int16),
-            pltpu.VMEM((sources, foot_n), F32),
-            pltpu.VMEM((sources, foot_n), F32),
-            pltpu.VMEM((sources, foot_n), F32),
-            pltpu.VMEM((sources, foot_n), F32),
+            pltpu.VMEM((2, BLOCK, foot_n), F32),
+            pltpu.VMEM((2, BLOCK, foot_n), F32),
+            pltpu.VMEM((2, BLOCK, foot_n), F32),
+            pltpu.VMEM((2, BLOCK, foot_n), F32),
             pltpu.VMEM((2, nf * frames, voxels), BF16),
             pltpu.VMEM((2, 4 * BLOCK, depth), BF16),
             pltpu.VMEM((2, 2 * BLOCK, LANES), BF16),
             pltpu.VMEM((2, 4 * BLOCK, LANES), F32),
             pltpu.VMEM((2, 2 * BLOCK, LANES), F32),
+            pltpu.VMEM((2, BLOCK, LANES), F32),
             pltpu.SemaphoreType.DMA((5,)),
             pltpu.SemaphoreType.DMA((3, nf)),
             pltpu.SemaphoreType.DMA((3, nf)),

time: 11.9 us -> 12 us (level)
  no operation moved by 1% of the time
where the time goes in v2:
time: 12 us; the launch traced here: 11.8 us
  Pallas kernels  11.2 us (93%)
  local copies, waits for them, and re-layouts  0.66 us (6%)
    pallas_call x1, Pallas kernels, local(): pl.pallas_call(functools.partial(kernel, nf, ns), out_shape=pltpu.VMEM((s...  11.2 us
    unnamed x1, local copies, waits for them, and re-layouts  0.66 us

profile of v2, /device:TPU:1, one launch (start us, length us, event | category | flops | bytes accessed | tf_op | source)
XLA Modules:
  0.0 11.8 jit_solution(5107477544718848245)
XLA Ops:
  0.0 11.2 %shard_map.55 = f32[16,2048]{1,0:T(8,128)S(1)} custom-call(s32[2]{0:T(128)} %order_in.1, bf16[8,2048]{1,0:T(8,128)(2,1)} %movie_in.1, bf16[8,16]{1,0:T(8,128)(2,1)} %traces_in.1, s32[16,2048]{1,0:T(8,128)} %index_in.1, f32[16,2048]{1,0:T(8,128)} %foot_in.1), custom_call_target="tpu_custom_call" | custom-call | flops 536870912 | bytes 500000 | tf_op jit(solution)/shard_map/pallas_call | solution.py:406
  11.2 0.7 %copy.7 = f32[16,2048]{1,0:T(8,128)} copy(f32[16,2048]{1,0:T(8,128)S(1)} %shard_map.55) | data formatting | bytes 262144

commit v3 on v2

--- a/solution.py
+++ b/solution.py
@@ -65,8 +65,8 @@
     pairs = ((index_in, index_ref), (foot_in, foot_ref), (order_in, order_ref),
              (movie_in, movie_ref), (traces_in, traces_ref))
     loads = [pltpu.make_async_copy(a, b, load_sem.at[i]) for i, (a, b) in enumerate(pairs)]
-    for load in loads:
-        load.start()
+    for i in (3, 4, 1, 0, 2):
+        loads[i].start()
 
     loads[3].wait()
     loads[4].wait()
@@ -178,7 +178,7 @@
         for k in range(BLOCK):
             scatter_row(k)
 
-            if k == BLOCK // 2 - 1:
+            if k == 0:
                 @pl.when(b == 0)
                 def _():
                     count = nf - 1 + nf * has_l.astype(jnp.int32) + nf * has_r.astype(jnp.int32)

time: 12 us -> 12.3 us (1.025)
  the two profiles are of different devices: /device:TPU:1 before, /device:TPU:0 now
where the time goes in v3:
time: 12.3 us; the launch traced here: 12.2 us
  Pallas kernels  11.5 us (93%)
  local copies, waits for them, and re-layouts  0.66 us (5%)
    pallas_call x1, Pallas kernels, local(): pl.pallas_call(functools.partial(kernel, nf, ns), out_shape=pltpu.VMEM((s...  11.5 us
    unnamed x1, local copies, waits for them, and re-layouts  0.66 us

profile of v3, /device:TPU:0, one launch (start us, length us, event | category | flops | bytes accessed | tf_op | source)
XLA Modules:
  0.0 12.2 jit_solution(17002466039985230662)
XLA Ops:
  0.0 11.5 %shard_map.55 = f32[16,2048]{1,0:T(8,128)S(1)} custom-call(s32[2]{0:T(128)} %order_in.1, bf16[8,2048]{1,0:T(8,128)(2,1)} %movie_in.1, bf16[8,16]{1,0:T(8,128)(2,1)} %traces_in.1, s32[16,2048]{1,0:T(8,128)} %index_in.1, f32[16,2048]{1,0:T(8,128)} %foot_in.1), custom_call_target="tpu_custom_call" | custom-call | flops 536870912 | bytes 500000 | tf_op jit(solution)/shard_map/pallas_call | solution.py:406
  11.5 0.7 %copy.7 = f32[16,2048]{1,0:T(8,128)} copy(f32[16,2048]{1,0:T(8,128)S(1)} %shard_map.55) | data formatting | bytes 262144

commit v4 on v2

--- a/solution.py
+++ b/solution.py
@@ -178,7 +178,7 @@
         for k in range(BLOCK):
             scatter_row(k)
 
-            if k == BLOCK // 2 - 1:
+            if k == BLOCK - 1:
                 @pl.when(b == 0)
                 def _():
                     count = nf - 1 + nf * has_l.astype(jnp.int32) + nf * has_r.astype(jnp.int32)
@@ -309,9 +309,7 @@
 
     early = 1 - lax.rem(s, 2)
 
-    def one_side(i, carry):
-        side = jnp.where(i == 0, early, 1 - early)
-
+    def update_side(side):
         @pl.when(jnp.where(side == 0, s, ns - 1 - s) > 0)
         def _():
             for b in range(2):
@@ -360,6 +358,11 @@
         moved = change(cross, [state[0], state[2]], [new_f, state[2]])
         new_s = step(1, rest[8:16] - moved[0:8])
         done = (jnp.where(swap, new_s, new_f), jnp.where(swap, new_f, new_s))
+        return done
+
+    done_early = update_side(early)
+    done_late = update_side(1 - early)
+    for side, done in ((early, done_early), (1 - early, done_late)):
         for b in range(2):
             for j in range(tiles):
                 at = (slice(b * BLOCK, (b + 1) * BLOCK), slice(j * LANES, (j + 1) * LANES))
@@ -372,9 +375,6 @@
                     got = jnp.take_along_axis(tile, lane, axis=1, mode="promise_in_bounds")
                     taken = jnp.where(chunk == c, got, taken)
                 out_ref[at] = taken
-        return carry
-
-    lax.fori_loop(0, 2, one_side, 0)
 
     for d in range(1, nf):
         peer(d).wait_send()

time: 12 us -> 11.6 us (0.967)
  Pallas kernels: 11.2 us -> 10.8 us
    pallas_call x1, Pallas kernels: 11.2 us -> 10.8 us  [local(): pl.pallas_call(functools.partial(kernel, nf, ns), out_shape=pltpu.VMEM((s...]
where the time goes in v4:
time: 11.6 us; the launch traced here: 11.5 us
  Pallas kernels  10.8 us (93%)
  local copies, waits for them, and re-layouts  0.66 us (6%)
    pallas_call x1, Pallas kernels, local(): pl.pallas_call(functools.partial(kernel, nf, ns), out_shape=pltpu.VMEM((s...  10.8 us
    unnamed x1, local copies, waits for them, and re-layouts  0.66 us

profile of v4, /device:TPU:1, one launch (start us, length us, event | category | flops | bytes accessed | tf_op | source)
XLA Modules:
  0.0 11.5 jit_solution(15437350108293751288)
XLA Ops:
  0.0 10.8 %shard_map.55 = f32[16,2048]{1,0:T(8,128)S(1)} custom-call(s32[2]{0:T(128)} %order_in.1, bf16[8,2048]{1,0:T(8,128)(2,1)} %movie_in.1, bf16[8,16]{1,0:T(8,128)(2,1)} %traces_in.1, s32[16,2048]{1,0:T(8,128)} %index_in.1, f32[16,2048]{1,0:T(8,128)} %foot_in.1), custom_call_target="tpu_custom_call" | custom-call | flops 536870912 | bytes 500000 | tf_op jit(solution)/shard_map/pallas_call | solution.py:406
  10.8 0.7 %copy.7 = f32[16,2048]{1,0:T(8,128)} copy(f32[16,2048]{1,0:T(8,128)S(1)} %shard_map.55) | data formatting | bytes 262144

commit v5 on v4

--- a/solution.py
+++ b/solution.py
@@ -31,8 +31,8 @@
 
 def kernel(
     nf, ns, order_in, movie_in, traces_in, index_in, foot_in, out_ref,
-    order_ref, movie_ref, traces_ref, index_ref, foot_ref, own, left, right, dense, sent, near,
-    hi_s, lo_s, vh_s, vl_s, movie_s, w_s, c_s, inv_s, size_s, unit_s,
+    order_ref, movie_ref, traces_ref, index_ref, foot_ref, own, margins, dense, sent, near,
+    hi_s, lo_s, vh_s, vl_s, unit_s,
     load_sem, send_m, recv_m, send_d, recv_d,
 ):
     f = lax.axis_index("frames")
@@ -79,12 +79,12 @@
 
     @pl.when(jnp.logical_not(has_l))
     def _():
-        left[...] = jnp.zeros_like(left)
+        margins[0] = jnp.zeros(margins.shape[1:], BF16)
         near[0] = jnp.full(near.shape[1:], -1, jnp.int32).astype(jnp.int16)
 
     @pl.when(jnp.logical_not(has_r))
     def _():
-        right[...] = jnp.zeros_like(right)
+        margins[1] = jnp.zeros(margins.shape[1:], BF16)
         near[1] = jnp.full(near.shape[1:], -1, jnp.int32).astype(jnp.int16)
 
     for load in loads[:3]:
@@ -126,14 +126,14 @@
     def to_right(d):
         to = lax.rem(f + d, nf)
         return pltpu.make_async_remote_copy(
-            src_ref=own.at[f, :, pl.ds(quarter, quarter + LANES)], dst_ref=left.at[f],
+            src_ref=own.at[f, :, pl.ds(quarter, quarter + LANES)], dst_ref=margins.at[0, f],
             send_sem=send_m.at[1, to], recv_sem=recv_m.at[1, f],
             device_id=(to, s + 1), device_id_type=MESH)
 
     def to_left(d):
         to = lax.rem(f + d, nf)
         return pltpu.make_async_remote_copy(
-            src_ref=own.at[f, :, pl.ds(0, quarter + LANES)], dst_ref=right.at[f],
+            src_ref=own.at[f, :, pl.ds(0, quarter + LANES)], dst_ref=margins.at[1, f],
             send_sem=send_m.at[2, to], recv_sem=recv_m.at[2, f],
             device_id=(to, s - 1), device_id_type=MESH)
 
@@ -220,35 +220,17 @@
             recv_sem=recv_m.at[0, lax.rem(f + d, nf)], device_id=(f, s),
             device_id_type=MESH).wait_recv()
 
-    @pl.when(has_l)
-    def _():
-        for d in range(nf):
-            pltpu.make_async_remote_copy(
-                src_ref=left.at[d], dst_ref=left.at[d], send_sem=send_m.at[1, 0],
-                recv_sem=recv_m.at[1, d], device_id=(f, s), device_id_type=MESH).wait_recv()
-
-    @pl.when(has_r)
-    def _():
-        for d in range(nf):
-            pltpu.make_async_remote_copy(
-                src_ref=right.at[d], dst_ref=right.at[d], send_sem=send_m.at[2, 0],
-                recv_sem=recv_m.at[2, d], device_id=(f, s), device_id_type=MESH).wait_recv()
-
     def all_frames(pick):
         return jnp.concatenate([pick(g) for g in range(nf)], axis=0)
 
-    def unpacked(ref, at):
+    def unpacked(load):
         def one(g):
-            both = ref[g, :, at:at + quarter].astype(F32)
+            both = load(g).astype(F32)
             return jnp.concatenate([both[:frames], both[frames:]], axis=1)
         return all_frames(one)
 
-    def trace_rows(ref, at):
-        return lambda g: ref[g, :, at:at + LANES].astype(F32)[:frames]
-
-    movie_l = jnp.concatenate([unpacked(left, LANES), unpacked(own, 0)], axis=1).astype(BF16)
-    movie_r = jnp.concatenate(
-        [unpacked(own, quarter + LANES), unpacked(right, 0)], axis=1).astype(BF16)
+    own_l = unpacked(lambda g: own[g, :, 0:quarter])
+    own_r = unpacked(lambda g: own[g, :, quarter + LANES:])
     total = nf * frames
     padding = jnp.zeros((LANES - total, LANES), F32)
     eye = (lax.broadcasted_iota(jnp.int32, (rows16, LANES), 0)
@@ -260,9 +242,7 @@
         return jnp.concatenate([jnp.where(swap, rows[BLOCK:], rows[:BLOCK]),
                                 jnp.where(swap, rows[:BLOCK], rows[BLOCK:])], axis=0)
 
-    t_own = by_source(trace_rows(own, quarter))
-    t_left = by_source(trace_rows(left, 0))
-    t_right = by_source(trace_rows(right, quarter))
+    t_own = by_source(lambda g: own[g, :, quarter:quarter + LANES].astype(F32)[:frames])
 
     depth = -(-(total + 3 * 32) // LANES) * LANES
     identity = (lax.broadcasted_iota(jnp.int32, (total, LANES), 0)
@@ -292,25 +272,43 @@
         inverse = 1.0 / (jnp.sum(t32 * t32, axis=1, keepdims=True) + 1.0)
         return first, second, inverse
 
-    for side, (movie, t_near) in enumerate(((movie_l, t_left), (movie_r, t_right))):
-        w, c, inverse = weights(t_near)
-        movie_s[side] = movie
-        w_s[side] = w
-        c_s[side] = c
-        inv_s[side] = jnp.broadcast_to(inverse, (4 * BLOCK, LANES))
-        block = ((left, 0), (right, quarter))[side]
-        scales = block[0][0, :, block[1]:block[1] + LANES].astype(F32)[frames:] * (1.0 / STEPS)
-        size_s[side] = jnp.concatenate(
+    tiles = foot_n // LANES
+    out_ref[...] = jnp.zeros_like(out_ref)
+
+    early = 1 - lax.rem(s, 2)
+
+    def update_side(side):
+        present = jnp.where(side == 0, s, ns - 1 - s) > 0
+
+        @pl.when(present)
+        def _():
+            for d in range(nf):
+                pltpu.make_async_remote_copy(
+                    src_ref=margins.at[side, d], dst_ref=margins.at[side, d],
+                    send_sem=send_m.at[0, 0], recv_sem=recv_m.at[1 + side, d],
+                    device_id=(f, s), device_id_type=MESH).wait_recv()
+
+        def wide(ref, at, start):
+            return jnp.concatenate(
+                [ref[at, (start + c) * BLOCK:(start + c + 1) * BLOCK, :] for c in range(half)],
+                axis=1)
+
+        def margin_part(g, first, last, width):
+            return jnp.where(side == 0, margins[side, g, :, first:first + width].astype(F32),
+                             margins[side, g, :, last:last + width].astype(F32))
+
+        outer = unpacked(lambda g: margin_part(g, LANES, 0, quarter))
+        movie = jnp.where(side == 0, jnp.concatenate([outer, own_l], axis=1),
+                          jnp.concatenate([own_r, outer], axis=1)).astype(BF16)
+        w, cross, inverse = weights(
+            by_source(lambda g: margin_part(g, 0, quarter, LANES)[:frames]))
+        w = w[:, :total + 96]
+        cross = cross[:, :48]
+        scales = margin_part(0, 0, quarter, LANES)[frames:] * (1.0 / STEPS)
+        size = jnp.concatenate(
             [jnp.broadcast_to(scales[:, 0:1], (BLOCK, LANES)),
              jnp.broadcast_to(scales[:, LANES // 2:LANES // 2 + 1], (BLOCK, LANES))], axis=0)
-
-    tiles = foot_n // LANES
-    out_ref[...] = jnp.zeros_like(out_ref)
-
-    early = 1 - lax.rem(s, 2)
-
-    def update_side(side):
-        @pl.when(jnp.where(side == 0, s, ns - 1 - s) > 0)
+        @pl.when(present)
         def _():
             for b in range(2):
                 pltpu.make_async_remote_copy(
@@ -319,17 +317,7 @@
                     send_sem=send_d.at[0, 0], recv_sem=recv_d.at[side, b],
                     device_id=(f, s), device_id_type=MESH).wait_recv()
 
-        def wide(ref, at, start):
-            return jnp.concatenate(
-                [ref[at, (start + c) * BLOCK:(start + c + 1) * BLOCK, :] for c in range(half)],
-                axis=1)
-
-        movie = movie_s[side]
-        w = w_s[side][:, :total + 96]
-        cross = c_s[side][:, :48]
-        inverse = inv_s[side][:, 0:1]
         steps = near[side].astype(jnp.int32).astype(F32).reshape(2, half, BLOCK, LANES)
-        size = size_s[side]
         enc = [wide(dense, side, 0), wide(dense, 2 + side, 0)]
         for b in range(2):
             enc.append(jnp.concatenate(
@@ -401,7 +389,6 @@
     sources, foot_n = footprint.shape
     margin = voxels // 2
     chunks = 2 * voxels // LANES
-    depth = -(-(nf * frames + 3 * 32) // LANES) * LANES
     vmem = pl.BlockSpec(memory_space=pltpu.VMEM)
     return pl.pallas_call(
         functools.partial(kernel, nf, ns),
@@ -415,8 +402,7 @@
             pltpu.VMEM(voxel_index.shape, voxel_index.dtype),
             pltpu.VMEM(footprint.shape, footprint.dtype),
             pltpu.VMEM((nf, 2 * frames, margin + LANES), BF16),
-            pltpu.VMEM((nf, 2 * frames, margin // 2 + LANES), BF16),
-            pltpu.VMEM((nf, 2 * frames, margin // 2 + LANES), BF16),
+            pltpu.VMEM((2, nf, 2 * frames, margin // 2 + LANES), BF16),
             pltpu.VMEM((4, BLOCK * chunks // 2, LANES), F32),
             pltpu.VMEM((4, BLOCK * chunks // 2, LANES), jnp.int16),
             pltpu.VMEM((2, BLOCK * chunks, LANES), jnp.int16),
@@ -424,11 +410,6 @@
             pltpu.VMEM((2, BLOCK, foot_n), F32),
             pltpu.VMEM((2, BLOCK, foot_n), F32),
             pltpu.VMEM((2, BLOCK, foot_n), F32),
-            pltpu.VMEM((2, nf * frames, voxels), BF16),
-            pltpu.VMEM((2, 4 * BLOCK, depth), BF16),
-            pltpu.VMEM((2, 2 * BLOCK, LANES), BF16),
-            pltpu.VMEM((2, 4 * BLOCK, LANES), F32),
-            pltpu.VMEM((2, 2 * BLOCK, LANES), F32),
             pltpu.VMEM((2, BLOCK, LANES), F32),
             pltpu.SemaphoreType.DMA((5,)),
             pltpu.SemaphoreType.DMA((3, nf)),

time: 11.6 us -> 11.2 us (0.966)
  the two profiles are of different devices: /device:TPU:1 before, /device:TPU:0 now
where the time goes in v5:
time: 11.2 us; the launch traced here: 11.1 us
  Pallas kernels  10.4 us (93%)
  local copies, waits for them, and re-layouts  0.66 us (6%)
    pallas_call x1, Pallas kernels, local(): pl.pallas_call(functools.partial(kernel, nf, ns), out_shape=pltpu.VMEM((s...  10.4 us
    unnamed x1, local copies, waits for them, and re-layouts  0.66 us

profile of v5, /device:TPU:0, one launch (start us, length us, event | category | flops | bytes accessed | tf_op | source)
XLA Modules:
  0.0 11.1 jit_solution(16770556277222538112)
XLA Ops:
  0.0 10.4 %shard_map.55 = f32[16,2048]{1,0:T(8,128)S(1)} custom-call(s32[2]{0:T(128)} %order_in.1, bf16[8,2048]{1,0:T(8,128)(2,1)} %movie_in.1, bf16[8,16]{1,0:T(8,128)(2,1)} %traces_in.1, s32[16,2048]{1,0:T(8,128)} %index_in.1, f32[16,2048]{1,0:T(8,128)} %foot_in.1), custom_call_target="tpu_custom_call" | custom-call | flops 536870912 | bytes 500000 | tf_op jit(solution)/shard_map/pallas_call | solution.py:393
  10.4 0.7 %copy.7 = f32[16,2048]{1,0:T(8,128)} copy(f32[16,2048]{1,0:T(8,128)S(1)} %shard_map.55) | data formatting | bytes 262144

commit v6 on v5

--- a/solution.py
+++ b/solution.py
@@ -178,7 +178,7 @@
         for k in range(BLOCK):
             scatter_row(k)
 
-            if k == BLOCK - 1:
+            if k == BLOCK - 3:
                 @pl.when(b == 0)
                 def _():
                     count = nf - 1 + nf * has_l.astype(jnp.int32) + nf * has_r.astype(jnp.int32)

time: 11.2 us -> 11.2 us (level)
  the two profiles are of different devices: /device:TPU:0 before, /device:TPU:1 now
where the time goes in v6:
time: 11.2 us; the launch traced here: 11.1 us
  Pallas kernels  10.4 us (93%)
  local copies, waits for them, and re-layouts  0.66 us (6%)
    pallas_call x1, Pallas kernels, local(): pl.pallas_call(functools.partial(kernel, nf, ns), out_shape=pltpu.VMEM((s...  10.4 us
    unnamed x1, local copies, waits for them, and re-layouts  0.66 us

profile of v6, /device:TPU:1, one launch (start us, length us, event | category | flops | bytes accessed | tf_op | source)
XLA Modules:
  0.0 11.1 jit_solution(10424638013350970815)
XLA Ops:
  0.0 10.4 %shard_map.55 = f32[16,2048]{1,0:T(8,128)S(1)} custom-call(s32[2]{0:T(128)} %order_in.1, bf16[8,2048]{1,0:T(8,128)(2,1)} %movie_in.1, bf16[8,16]{1,0:T(8,128)(2,1)} %traces_in.1, s32[16,2048]{1,0:T(8,128)} %index_in.1, f32[16,2048]{1,0:T(8,128)} %foot_in.1), custom_call_target="tpu_custom_call" | custom-call | flops 536870912 | bytes 500000 | tf_op jit(solution)/shard_map/pallas_call | solution.py:393
  10.4 0.7 %copy.7 = f32[16,2048]{1,0:T(8,128)} copy(f32[16,2048]{1,0:T(8,128)S(1)} %shard_map.55) | data formatting | bytes 262144
